TPU v7x, 512 devices: a whole 4x8x8 slice. The times are simulated.
512 devices in a mesh: tok: 64 (over x, y, core), col: 8 (over z).
Axes of the slice: x: 4, y: 8, z: 8, core: 2. Of those that a mesh axis runs over, the one named last changes fastest.
Arguments:
- acts: bfloat16 [65536, 18432], P('tok', 'col'), may hold values from -16 to 16
- basis: bfloat16 [65536, 256], P('tok'), may hold values from -0.0234375 to 0.0234375
Outputs:
- corange: bfloat16 [18432, 256], P('col')
- range_next: bfloat16 [65536, 256], P('tok')
All inputs are finite; a program needn't handle non-finite values.
Results may differ from a plain program's by a relative error of at most 0.0046.
Values may be sent and summed in bfloat16 or wider, within the bound.
No kernel may reach another device: no remote copies, remote signals or barrier semaphores. Data moves between devices by JAX's collectives and lax.ppermute only.
A program may use at most 64 MiB of HBM per device.

v0:
```python
import math

import jax
import jax.numpy as jnp
from jax import lax
from jax.sharding import PartitionSpec as P

N = 18432


def contract_tokens(block, basis):
    return lax.dot_general(
        block, basis, (((0,), (0,)), ((), ())), preferred_element_type=jnp.float32
    )


def on_device(acts, basis):
    partial_b = contract_tokens(acts, basis)
    corange = lax.psum(partial_b, "tok").astype(jnp.bfloat16)
    partial_y = jnp.dot(acts, corange, preferred_element_type=jnp.float32)
    summed = lax.psum(partial_y, "col")
    range_next = (summed * (1.0 / math.sqrt(N))).astype(jnp.bfloat16)
    return (corange, range_next)


def solution(mesh):
    in_specs = (P("tok", "col"), P("tok", None))
    out_specs = (P("col", None), P("tok", None))
    return jax.shard_map(
        on_device, mesh=mesh, in_specs=in_specs, out_specs=out_specs, check_vma=False
    )
```

profile of v0, /device:TPU:1, one launch (start us, length us, event | category | flops | bytes accessed | tf_op | source)
XLA Modules:
  0.0 377.8 jit_solution(5437206772514119297)
XLA Ops:
  7.2 0.0 copy-start
  7.2 0.0 all-reduce.3.cloned.1.call-start
  7.2 1.0 copy-done
  8.2 3.8 fusion
  12.0 271.1 %all-reduce.4 = bf16[2304,256]{1,0:T(8,128)(2,1)} all-reduce(f32[2304,256]{1,0:T(8,128)S(1)} %fusion), channel_id=1, replica_groups=mesh['tok'=64,'col'=8] {'tok'}, use_global_device_ids=true, to_apply=%region_0.0 | all-reduce | flops 589824 | bytes 3538944 | tf_op jit(solution)/shard_map/psum | solution.py:19
  283.1 5.2 %convolution_bitcast_fusion = f32[1024,256]{0,1:T(8,128)} fusion(bf16[2304,256]{1,0:T(8,128)(2,1)} %all-reduce.4, bf16[1024,2304]{1,0:T(8,128)(2,1)} %param.2), kind=kOutput, calls=%fused_computation | convolution fusion | flops 1207959552 | bytes 6946816 | tf_op jit(solution)/shard_map/dot_general | solution.py:20
  288.3 0.0 all-reduce.3.cloned.1.call-update
  288.3 80.4 %all-reduce.3.cloned.1.call-done = f32[1024,256]{0,1:T(8,128)} async-done(((f32[1024,256]{0,1:T(8,128)}), f32[1024,256]{0,1:T(8,128)}) %all-reduce.3.cloned.1.call-update) | async-done | bytes 1048592 | tf_op jit(solution)/shard_map/psum | solution.py:21
  368.7 1.3 multiply_convert_fusion
  370.0 1.0 copy.4
Async XLA Ops:
  7.2 1.0 copy-start
  7.2 361.5 %all-reduce.3.cloned.1.call-start = ((), (), s32[]{:S(2)}) async-start(), calls=%async_computation | async-start | bytes 2097152 | tf_op jit(solution)/shard_map/psum | solution.py:21
Sparse Core Ops, SparseCore 0:
  288.4 80.2 all-reduce.2
where the time goes:
time: 381 us; the launch traced here: 378 us
  blocking collectives  271 us (71%)
  waiting for transfers between devices  80.4 us (21%)
  between operations  14 us (4%)
  matrix products  8.94 us (2%)
    psum x1, blocking collectives, on_device(): corange = lax.psum(partial_b, 'tok').astype(jnp.bfloat16)  271 us
    psum x1, waiting for transfers between devices, on_device(): summed = lax.psum(partial_y, 'col')  80.4 us
  transfers between devices with their start and end apart: 1, of which 1 were waited for; matrix products, arithmetic and copies ran while one was open for 0% of the time, Pallas kernels for 0%

commit v1 on v0

v1 whole, which is shorter than its diff:
```python
import math

import jax
import jax.numpy as jnp
from jax import lax
from jax.sharding import Mesh, PartitionSpec as P

N = 18432
XY = ("x", "y")
SWAP = ((0, 1), (1, 0))


def contract_tokens(block, basis):
    return lax.dot_general(
        block, basis, (((0,), (0,)), ((), ())), preferred_element_type=jnp.float32
    )


def exchange_sum(pieces, axes):
    landed = lax.all_to_all(pieces, axes, 0, 0)
    return jnp.sum(landed.astype(jnp.float32), axis=0)


def share(piece, axes, n):
    return lax.all_to_all(jnp.broadcast_to(piece[None], (n,) + piece.shape), axes, 0, 0)


def on_device(acts, basis):
    rows, cols = acts.shape
    k = basis.shape[1]
    half = k // 2
    core = lax.axis_index("core")
    own = core * half
    other = half - own

    partial_b = contract_tokens(acts, basis)
    to_other = lax.dynamic_slice(partial_b, (0, other), (cols, half)).astype(jnp.bfloat16)
    kept = lax.dynamic_slice(partial_b, (0, own), (cols, half))
    from_other = lax.ppermute(to_other, "core", SWAP)
    chip_sum = (kept + from_other.astype(jnp.float32)).astype(jnp.bfloat16)

    piece = exchange_sum(chip_sum.reshape(32, cols // 32, half), XY).astype(jnp.bfloat16)
    mine = share(piece, XY, 32).reshape(cols, half)
    theirs = lax.ppermute(mine, "core", SWAP)
    first = jnp.where(core == 0, mine, theirs)
    second = jnp.where(core == 0, theirs, mine)
    corange = jnp.concatenate([first, second], axis=1)

    partial_y = jnp.dot(acts, corange, preferred_element_type=jnp.float32).astype(jnp.bfloat16)
    summed = exchange_sum(partial_y.reshape(8, rows // 8, k), "z")
    scaled = (summed * (1.0 / math.sqrt(N))).astype(jnp.bfloat16)
    range_next = share(scaled, "z", 8).reshape(rows, k)
    return (corange, range_next)


def solution(mesh):
    fine = Mesh(mesh.devices.reshape(4, 8, 2, 8), ("x", "y", "core", "z"))
    tok = ("x", "y", "core")
    in_specs = (P(tok, "z"), P(tok, None))
    out_specs = (P("z", None), P(tok, None))
    return jax.shard_map(
        on_device, mesh=fine, in_specs=in_specs, out_specs=out_specs, check_vma=False
    )
```

time: 381 us -> 120 us (0.31)
  blocking collectives: 271 us -> 91.4 us
  waiting for transfers between devices: 80.4 us -> 3.41 us
  starting transfers between devices: 0.04 us -> 14.6 us
  between operations: 14 us -> 0.76 us
    psum x1 -> x0, blocking collectives: 271 us -> none  [on_device(): corange = lax.psum(partial_b, 'tok').astype(jnp.bfloat16)]
    all_to_all x0 -> x4, blocking collectives: none -> 91.4 us  [the longest x2 47.5 us: exchange_sum(): landed = lax.all_to_all(pieces, axes, 0, 0)]
    psum x1 -> x0, waiting for transfers between devices: 80.4 us -> none  [on_device(): summed = lax.psum(partial_y, 'col')]
    ppermute x0 -> x2, starting transfers between devices: none -> 14.6 us  [the longest x1 8.78 us: on_device(): from_other = lax.ppermute(to_other, 'core', SWAP)]
  transfers between devices with their start and end apart: 1 -> 2, of which waited for: 1 -> 2; matrix products, arithmetic and copies ran while one was open for 0% -> 0% of each run, Pallas kernels for 0% -> 0%
where the time goes in v1:
time: 120 us; the launch traced here: 119 us
  blocking collectives  91.4 us (76%)
  starting transfers between devices  14.6 us (12%)
  matrix products  5.2 us (4%)
  local copies, waits for them, and re-layouts  3.53 us (3%)
  waiting for transfers between devices  3.41 us (3%)
    all_to_all x2, blocking collectives, exchange_sum(): landed = lax.all_to_all(pieces, axes, 0, 0)  47.5 us
    all_to_all x2, blocking collectives, share(): lax.all_to_all(jnp.broadcast_to(piece[None], (n,) + piece.shape), axes, 0...  43.9 us
    ppermute x1, starting transfers between devices, on_device(): from_other = lax.ppermute(to_other, 'core', SWAP)  8.78 us
    ppermute x1, starting transfers between devices, on_device(): theirs = lax.ppermute(mine, 'core', SWAP)  5.84 us
    dot_general x1, matrix products, contract_tokens(): lax.dot_general(block, basis, (((0,), (0,)), ((), ())), preferred_element...  3.77 us
  transfers between devices with their start and end apart: 2, of which 2 were waited for; matrix products, arithmetic and copies ran while one was open for 0% of the time, Pallas kernels for 0%

profile of v1, /device:TPU:1, one launch (start us, length us, event | category | flops | bytes accessed | tf_op | source)
XLA Modules:
  0.0 119.5 jit_solution(12074060618035742280)
XLA Ops:
  0.6 0.0 copy-start
  0.7 1.0 copy-done
  1.7 3.8 %fusion.1 = f32[2304,256]{1,0:T(8,128)S(1)} fusion(bf16[1024,2304]{1,0:T(8,128)(2,1)} %param.2, bf16[1024,256]{1,0:T(8,128)(2,1)S(1)} %copy-done), kind=kOutput, calls=%fused_computation.10 | convolution fusion | flops 1207959552 | bytes 7602176 | tf_op jit(solution)/shard_map/dot_general | solution.py:14
  5.4 0.9 dynamic-slice_convert_fusion
  6.4 8.8 %collective-permute-start = (bf16[2304,128]{1,0:T(8,128)(2,1)}, bf16[2304,128]{1,0:T(8,128)(2,1)S(1)}, u32[]{:S(2)}, u32[]{:S(2)}) collective-permute-start(bf16[2304,128]{1,0:T(8,128)(2,1)} %dynamic-slice_convert_fusion), channel_id=1, source_target_pairs={{0,8},{8,0},{1,9},{9,1},{2,10},{10,2},{3,11},{11,3},{4,12},{12,4},... | collective-permute-start | bytes 1769480 | tf_op jit(solution)/shard_map/ppermute | solution.py:39
  15.1 1.8 %collective-permute-done = bf16[2304,128]{1,0:T(8,128)(2,1)S(1)} collective-permute-done((bf16[2304,128]{1,0:T(8,128)(2,1)}, bf16[2304,128]{1,0:T(8,128)(2,1)S(1)}, u32[]{:S(2)}, u32[]{:S(2)}) %collective-permute-start) | collective-permute-done | bytes 589856 | tf_op jit(solution)/shard_map/ppermute | solution.py:39
  17.0 0.1 add_convert_fusion
  17.1 19.6 %all_to_all.20 = bf16[32,72,128]{2,1,0:T(8,128)(2,1)S(1)} all-to-all(bf16[32,72,128]{2,1,0:T(8,128)(2,1)S(1)} %bitcast.16), channel_id=1, replica_groups=mesh['x'=4,'y'=8,'core'=2,'z'=8] {'x','y'}, dimensions={0} | all-to-all | bytes 1179648 | tf_op jit(solution)/shard_map/all_to_all | solution.py:20
  36.7 0.1 reduce_sum.21
  36.8 0.1 broadcast_in_dim.4
  36.9 23.7 %all_to_all.21 = bf16[32,72,128]{2,1,0:T(8,128)(2,1)S(1)} all-to-all(bf16[32,72,128]{2,1,0:T(8,128)(2,1)S(1)} %broadcast_in_dim.4), channel_id=1, replica_groups=mesh['x'=4,'y'=8,'core'=2,'z'=8] {'x','y'}, dimensions={0} | all-to-all | bytes 1179648 | tf_op jit(solution)/shard_map/all_to_all | solution.py:25
  60.6 5.8 %collective-permute-start.1 = (bf16[2304,128]{1,0:T(8,128)(2,1)S(1)}, bf16[2304,128]{1,0:T(8,128)(2,1)S(1)}, u32[]{:S(2)}, u32[]{:S(2)}) collective-permute-start(bf16[2304,128]{1,0:T(8,128)(2,1)S(1)} %bitcast.15), channel_id=1, source_target_pairs={{0,8},{8,0},{1,9},{9,1},{2,10},{10,2},{3,11},{11,3},{4,12},{12,4},... | collective-permute-start | bytes 1769480 | tf_op jit(solution)/shard_map/ppermute | solution.py:44
  66.4 0.0 copy-start.2
  66.5 1.6 %collective-permute-done.1 = bf16[2304,128]{1,0:T(8,128)(2,1)S(1)} collective-permute-done((bf16[2304,128]{1,0:T(8,128)(2,1)S(1)}, bf16[2304,128]{1,0:T(8,128)(2,1)S(1)}, u32[]{:S(2)}, u32[]{:S(2)}) %collective-permute-start.1) | collective-permute-done | bytes 589856 | tf_op jit(solution)/shard_map/ppermute | solution.py:44
  68.0 0.1 broadcast_select_fusion.1
  68.2 0.1 pad_maximum_fusion
  68.3 0.5 copy-done.2
  68.8 0.0 copy-start.1
  68.8 1.4 %fusion = bf16[32,8,8,128]{3,2,1,0:T(8,128)(2,1)S(1)} fusion(bf16[2304,256]{1,0:T(8,128)(2,1)S(1)} %pad_maximum_fusion, bf16[1024,2304]{1,0:T(8,128)(2,1)S(1)} %copy-done.2), kind=kOutput, calls=%fused_computation.1 | convolution fusion | flops 1208221696 | bytes 6422528 | tf_op jit(solution)/shard_map/dot_general | solution.py:49
  70.2 0.0 copy-done.1
  70.2 0.1 copy.10
  70.3 27.8 %all_to_all.22 = bf16[8,128,256]{1,2,0:T(8,128)(2,1)S(1)} all-to-all(bf16[8,128,256]{1,2,0:T(8,128)(2,1)S(1)} %bitcast.17), channel_id=1, replica_groups=mesh['x'=4,'y'=8,'core'=2,'z'=8] {'z'}, dimensions={0} | all-to-all | bytes 1048576 | tf_op jit(solution)/shard_map/all_to_all | solution.py:20
  98.2 0.1 convert_reduce_fusion
  98.2 0.1 copy.6
  98.4 20.3 %all_to_all.23 = bf16[8,128,256]{2,1,0:T(8,128)(2,1)S(1)} all-to-all(bf16[8,128,256]{2,1,0:T(8,128)(2,1)S(1)} %broadcast_in_dim.5), channel_id=1, replica_groups=mesh['x'=4,'y'=8,'core'=2,'z'=8] {'z'}, dimensions={0} | all-to-all | bytes 1048576 | tf_op jit(solution)/shard_map/all_to_all | solution.py:25
  118.7 0.8 copy.12
  (2 shorter events, 0.1 us)
Async XLA Ops:
  0.6 1.0 copy-start
  6.4 10.6 %collective-permute-start = (bf16[2304,128]{1,0:T(8,128)(2,1)}, bf16[2304,128]{1,0:T(8,128)(2,1)S(1)}, u32[]{:S(2)}, u32[]{:S(2)}) collective-permute-start(bf16[2304,128]{1,0:T(8,128)(2,1)} %dynamic-slice_convert_fusion), channel_id=1, source_target_pairs={{0,8},{8,0},{1,9},{9,1},{2,10},{10,2},{3,11},{11,3},{4,12},{12,4},... | collective-permute-start | bytes 1769480 | tf_op jit(solution)/shard_map/ppermute | solution.py:39
  60.6 7.5 %collective-permute-start.1 = (bf16[2304,128]{1,0:T(8,128)(2,1)S(1)}, bf16[2304,128]{1,0:T(8,128)(2,1)S(1)}, u32[]{:S(2)}, u32[]{:S(2)}) collective-permute-start(bf16[2304,128]{1,0:T(8,128)(2,1)S(1)} %bitcast.15), channel_id=1, source_target_pairs={{0,8},{8,0},{1,9},{9,1},{2,10},{10,2},{3,11},{11,3},{4,12},{12,4},... | collective-permute-start | bytes 1769480 | tf_op jit(solution)/shard_map/ppermute | solution.py:44
  66.4 2.3 %copy-start.2 = (bf16[1024,2304]{1,0:T(8,128)(2,1)S(1)}, bf16[1024,2304]{1,0:T(8,128)(2,1)}, u32[]{:S(2)}) copy-start(bf16[1024,2304]{1,0:T(8,128)(2,1)} %param.2) | copy-start | bytes 14155780
  68.8 1.4 %copy-start.1 = (bf16[2304,256]{1,0:T(8,128)(2,1)}, bf16[2304,256]{1,0:T(8,128)(2,1)S(1)}, u32[]{:S(2)}) copy-start(bf16[2304,256]{1,0:T(8,128)(2,1)S(1)} %pad_maximum_fusion) | copy-start | bytes 3538948

commit v2 on v1

v2 whole, which is shorter than its diff:
```python
import math

import jax
import jax.numpy as jnp
import numpy as np
from jax import lax
from jax.sharding import Mesh, PartitionSpec as P

N = 18432
SWAP = ((0, 1), (1, 0))
F32, BF16 = jnp.float32, jnp.bfloat16
AXES = ("x", "y", "core", "z")
SIZES = (4, 8, 2, 8)
IDS = np.arange(512).reshape(SIZES)


def xy_groups():
    order = [((p // 8 + p) % 4, 3 * p % 8) for p in range(32)]
    return [
        [int(IDS[x, y, core, z]) for x, y in order] for core in range(2) for z in range(8)
    ]


def z_groups():
    return [
        [int(IDS[x, y, core, (5 if core else 3) * p % 8]) for p in range(8)]
        for x in range(4)
        for y in range(8)
        for core in range(2)
    ]


def exchange(pieces, groups):
    return lax.all_to_all(pieces, AXES, 0, 0, axis_index_groups=groups)


def exchange_sum(pieces, groups):
    return jnp.sum(exchange(pieces, groups).astype(F32), axis=0)


def share(piece, groups):
    n = len(groups[0])
    return exchange(jnp.broadcast_to(piece[None], (n,) + piece.shape), groups)


def on_device(acts, basis):
    rows, cols = acts.shape
    k = basis.shape[1]
    half = k // 2
    core = lax.axis_index("core").astype(jnp.int32)
    own = core * half
    other = half - own

    product = lax.dot_general(acts, basis, (((0,), (0,)), ((), ())), preferred_element_type=F32)
    to_other = lax.dynamic_slice(product, (0, other), (cols, half)).astype(BF16)
    kept = lax.dynamic_slice(product, (0, own), (cols, half))
    from_other = lax.ppermute(to_other, "core", SWAP)
    chip_sum = (kept + from_other.astype(F32)).astype(BF16)
    piece = exchange_sum(chip_sum.reshape(32, cols // 32, half), xy_groups()).astype(BF16)
    mine = share(piece, xy_groups()).reshape(cols, half)
    theirs = lax.ppermute(mine, "core", SWAP)
    first = jnp.where(core == 0, mine, theirs)
    second = jnp.where(core == 0, theirs, mine)
    corange = jnp.concatenate([first, second], axis=1)

    partial_y = jnp.dot(acts, corange, preferred_element_type=F32).astype(BF16)
    summed = exchange_sum(partial_y.reshape(8, rows // 8, k), z_groups())
    scaled = (summed * (1.0 / math.sqrt(N))).astype(BF16)
    range_next = share(scaled, z_groups()).reshape(rows, k)
    return (corange, range_next)


def solution(mesh):
    fine = Mesh(mesh.devices.reshape(SIZES), AXES)
    tok = ("x", "y", "core")
    in_specs = (P(tok, "z"), P(tok, None))
    out_specs = (P("z", None), P(tok, None))
    return jax.shard_map(
        on_device, mesh=fine, in_specs=in_specs, out_specs=out_specs, check_vma=False
    )
```

time: 120 us -> 116 us (0.967)
  blocking collectives: 91.4 us -> 85 us
  starting transfers between devices: 14.6 us -> 16.1 us
    all_to_all x4, blocking collectives: 91.4 us -> 85 us  [exchange(): return lax.all_to_all(pieces, AXES, 0, 0, axis_index_groups=groups)]
    ppermute x1, starting transfers between devices: 5.84 us -> 7.33 us  [on_device(): theirs = lax.ppermute(mine, 'core', SWAP)]
where the time goes in v2:
time: 116 us; the launch traced here: 115 us
  blocking collectives  85 us (73%)
  starting transfers between devices  16.1 us (14%)
  matrix products  5.2 us (4%)
  local copies, waits for them, and re-layouts  3.53 us (3%)
  waiting for transfers between devices  3.41 us (3%)
    all_to_all x4, blocking collectives, exchange(): return lax.all_to_all(pieces, AXES, 0, 0, axis_index_groups=groups)  85 us
    ppermute x1, starting transfers between devices, on_device(): from_other = lax.ppermute(to_other, 'core', SWAP)  8.78 us
    ppermute x1, starting transfers between devices, on_device(): theirs = lax.ppermute(mine, 'core', SWAP)  7.33 us
    dot_general x1, matrix products, on_device(): lax.dot_general(acts, basis, (((0,), (0,)), ((), ())), preferred_element_...  3.77 us
  transfers between devices with their start and end apart: 2, of which 2 were waited for; matrix products, arithmetic and copies ran while one was open for 0% of the time, Pallas kernels for 0%

profile of v2, /device:TPU:1, one launch (start us, length us, event | category | flops | bytes accessed | tf_op | source)
XLA Modules:
  0.0 114.6 jit_solution(6414639305272688603)
XLA Ops:
  0.6 0.0 copy-start
  0.7 1.0 copy-done
  1.7 3.8 %fusion.1 = f32[2304,256]{1,0:T(8,128)S(1)} fusion(bf16[1024,2304]{1,0:T(8,128)(2,1)} %param.2, bf16[1024,256]{1,0:T(8,128)(2,1)S(1)} %copy-done), kind=kOutput, calls=%fused_computation.10 | convolution fusion | flops 1207959552 | bytes 7602176 | tf_op jit(solution)/shard_map/dot_general | solution.py:54
  5.4 0.9 dynamic-slice_convert_fusion
  6.4 8.8 %collective-permute-start = (bf16[2304,128]{1,0:T(8,128)(2,1)}, bf16[2304,128]{1,0:T(8,128)(2,1)S(1)}, u32[]{:S(2)}, u32[]{:S(2)}) collective-permute-start(bf16[2304,128]{1,0:T(8,128)(2,1)} %dynamic-slice_convert_fusion), channel_id=1, source_target_pairs={{0,8},{8,0},{1,9},{9,1},{2,10},{10,2},{3,11},{11,3},{4,12},{12,4},... | collective-permute-start | bytes 1769480 | tf_op jit(solution)/shard_map/ppermute | solution.py:57
  15.1 1.8 %collective-permute-done = bf16[2304,128]{1,0:T(8,128)(2,1)S(1)} collective-permute-done((bf16[2304,128]{1,0:T(8,128)(2,1)}, bf16[2304,128]{1,0:T(8,128)(2,1)S(1)}, u32[]{:S(2)}, u32[]{:S(2)}) %collective-permute-start) | collective-permute-done | bytes 589856 | tf_op jit(solution)/shard_map/ppermute | solution.py:57
  17.0 0.1 add_convert_fusion
  17.1 20.3 %all_to_all.20 = bf16[32,72,128]{2,1,0:T(8,128)(2,1)S(1)} all-to-all(bf16[32,72,128]{2,1,0:T(8,128)(2,1)S(1)} %bitcast.16), channel_id=1, replica_groups={{0,176,352,400,64,240,288,464,128,304,480,16,192,368,416,80,256,432,96,..., dimensions={0} | all-to-all | bytes 1179648 | tf_op jit(solution)/shard_map/all_to_all | solution.py:34
  37.4 0.1 reduce_sum.21
  37.5 0.1 broadcast_in_dim.4
  37.5 21.2 %all_to_all.21 = bf16[32,72,128]{2,1,0:T(8,128)(2,1)S(1)} all-to-all(bf16[32,72,128]{2,1,0:T(8,128)(2,1)S(1)} %broadcast_in_dim.4), channel_id=1, replica_groups={{0,176,352,400,64,240,288,464,128,304,480,16,192,368,416,80,256,432,96,..., dimensions={0} | all-to-all | bytes 1179648 | tf_op jit(solution)/shard_map/all_to_all | solution.py:34
  58.7 7.3 %collective-permute-start.1 = (bf16[2304,128]{1,0:T(8,128)(2,1)S(1)}, bf16[2304,128]{1,0:T(8,128)(2,1)S(1)}, u32[]{:S(2)}, u32[]{:S(2)}) collective-permute-start(bf16[2304,128]{1,0:T(8,128)(2,1)S(1)} %bitcast.15), channel_id=1, source_target_pairs={{0,8},{8,0},{1,9},{9,1},{2,10},{10,2},{3,11},{11,3},{4,12},{12,4},... | collective-permute-start | bytes 1769480 | tf_op jit(solution)/shard_map/ppermute | solution.py:61
  66.0 0.0 copy-start.2
  66.1 1.6 %collective-permute-done.1 = bf16[2304,128]{1,0:T(8,128)(2,1)S(1)} collective-permute-done((bf16[2304,128]{1,0:T(8,128)(2,1)S(1)}, bf16[2304,128]{1,0:T(8,128)(2,1)S(1)}, u32[]{:S(2)}, u32[]{:S(2)}) %collective-permute-start.1) | collective-permute-done | bytes 589856 | tf_op jit(solution)/shard_map/ppermute | solution.py:61
  67.6 0.1 broadcast_select_fusion.1
  67.8 0.1 pad_maximum_fusion
  67.9 0.5 copy-done.2
  68.4 0.0 copy-start.1
  68.4 1.4 %fusion = bf16[32,8,8,128]{3,2,1,0:T(8,128)(2,1)S(1)} fusion(bf16[2304,256]{1,0:T(8,128)(2,1)S(1)} %pad_maximum_fusion, bf16[1024,2304]{1,0:T(8,128)(2,1)S(1)} %copy-done.2), kind=kOutput, calls=%fused_computation.1 | convolution fusion | flops 1208221696 | bytes 6422528 | tf_op jit(solution)/shard_map/dot_general | solution.py:66
  69.8 0.0 copy-done.1
  69.8 0.1 copy.10
  69.9 26.3 %all_to_all.22 = bf16[8,128,256]{1,2,0:T(8,128)(2,1)S(1)} all-to-all(bf16[8,128,256]{1,2,0:T(8,128)(2,1)S(1)} %bitcast.17), channel_id=1, replica_groups={{0,3,6,1,4,7,2,5},{8,13,10,15,12,9,14,11},{16,19,22,17,20,23,18,21},{24..., dimensions={0} | all-to-all | bytes 1048576 | tf_op jit(solution)/shard_map/all_to_all | solution.py:34
  96.2 0.1 convert_reduce_fusion
  96.3 0.1 copy.6
  96.5 17.3 %all_to_all.23 = bf16[8,128,256]{2,1,0:T(8,128)(2,1)S(1)} all-to-all(bf16[8,128,256]{2,1,0:T(8,128)(2,1)S(1)} %broadcast_in_dim.5), channel_id=1, replica_groups={{0,3,6,1,4,7,2,5},{8,13,10,15,12,9,14,11},{16,19,22,17,20,23,18,21},{24..., dimensions={0} | all-to-all | bytes 1048576 | tf_op jit(solution)/shard_map/all_to_all | solution.py:34
  113.8 0.8 copy.12
  (2 shorter events, 0.1 us)
Async XLA Ops:
  0.6 1.0 copy-start
  6.4 10.6 %collective-permute-start = (bf16[2304,128]{1,0:T(8,128)(2,1)}, bf16[2304,128]{1,0:T(8,128)(2,1)S(1)}, u32[]{:S(2)}, u32[]{:S(2)}) collective-permute-start(bf16[2304,128]{1,0:T(8,128)(2,1)} %dynamic-slice_convert_fusion), channel_id=1, source_target_pairs={{0,8},{8,0},{1,9},{9,1},{2,10},{10,2},{3,11},{11,3},{4,12},{12,4},... | collective-permute-start | bytes 1769480 | tf_op jit(solution)/shard_map/ppermute | solution.py:57
  58.7 8.9 %collective-permute-start.1 = (bf16[2304,128]{1,0:T(8,128)(2,1)S(1)}, bf16[2304,128]{1,0:T(8,128)(2,1)S(1)}, u32[]{:S(2)}, u32[]{:S(2)}) collective-permute-start(bf16[2304,128]{1,0:T(8,128)(2,1)S(1)} %bitcast.15), channel_id=1, source_target_pairs={{0,8},{8,0},{1,9},{9,1},{2,10},{10,2},{3,11},{11,3},{4,12},{12,4},... | collective-permute-start | bytes 1769480 | tf_op jit(solution)/shard_map/ppermute | solution.py:61
  66.0 2.3 %copy-start.2 = (bf16[1024,2304]{1,0:T(8,128)(2,1)S(1)}, bf16[1024,2304]{1,0:T(8,128)(2,1)}, u32[]{:S(2)}) copy-start(bf16[1024,2304]{1,0:T(8,128)(2,1)} %param.2) | copy-start | bytes 14155780
  68.4 1.4 %copy-start.1 = (bf16[2304,256]{1,0:T(8,128)(2,1)}, bf16[2304,256]{1,0:T(8,128)(2,1)S(1)}, u32[]{:S(2)}) copy-start(bf16[2304,256]{1,0:T(8,128)(2,1)S(1)} %pad_maximum_fusion) | copy-start | bytes 3538948

commit v3 on v2

--- a/solution.py
+++ b/solution.py
@@ -4,6 +4,8 @@
 import jax.numpy as jnp
 import numpy as np
 from jax import lax
+from jax.experimental import pallas as pl
+from jax.experimental.pallas import tpu as pltpu
 from jax.sharding import Mesh, PartitionSpec as P
 
 N = 18432
@@ -11,6 +13,10 @@
 F32, BF16 = jnp.float32, jnp.bfloat16
 AXES = ("x", "y", "core", "z")
 SIZES = (4, 8, 2, 8)
+LANES = 128
+VMEM_LIMIT = 54 * 1024 * 1024
+HOLD_LIMIT = 52 * 1024 * 1024
+HOLD_PARTS = 4
 IDS = np.arange(512).reshape(SIZES)
 
 
@@ -43,27 +49,98 @@
     return exchange(jnp.broadcast_to(piece[None], (n,) + piece.shape), groups)
 
 
+def half_product_kernel(start_ref, acts_hbm, basis_hbm, out_ref, block_ref, basis_ref, acts_sem, basis_sem):
+    groups, half, lanes = out_ref.shape
+    start = pl.multiple_of(start_ref[0], LANES)
+    basis_copy = pltpu.make_async_copy(basis_hbm, basis_ref, basis_sem)
+    acts_copy = pltpu.make_async_copy(acts_hbm.at[:, pl.ds(start, half)], block_ref, acts_sem)
+    basis_copy.start()
+    acts_copy.start()
+    basis_copy.wait()
+    basis = basis_ref[...].T
+    acts_copy.wait()
+    product = jnp.dot(basis, block_ref[...], preferred_element_type=F32)
+    turned = product.astype(out_ref.dtype).T
+    for g in range(groups):
+        out_ref[g] = turned[:, g * lanes : (g + 1) * lanes]
+
+
+def half_product(acts, basis, start, dtype):
+    rows, cols = acts.shape
+    k, half = basis.shape[1], cols // 2
+    vmem = pl.BlockSpec(memory_space=pltpu.VMEM)
+    hbm = pl.BlockSpec(memory_space=pl.ANY)
+    return pl.pallas_call(
+        half_product_kernel,
+        out_shape=pltpu.VMEM((k // LANES, half, LANES), dtype),
+        in_specs=[pl.BlockSpec(memory_space=pltpu.SMEM), hbm, hbm],
+        out_specs=vmem,
+        scratch_shapes=[
+            pltpu.VMEM((rows, half), BF16),
+            pltpu.VMEM((rows, k), BF16),
+            pltpu.SemaphoreType.DMA,
+            pltpu.SemaphoreType.DMA,
+        ],
+        compiler_params=pltpu.CompilerParams(vmem_limit_bytes=VMEM_LIMIT),
+        cost_estimate=pl.CostEstimate(
+            flops=2 * rows * half * k,
+            bytes_accessed=2 * rows * (half + k),
+            transcendentals=0,
+        ),
+    )(start.reshape(1), acts, basis)
+
+
+def side_by_side(groups):
+    return jnp.concatenate([groups[0], groups[1]], axis=1)
+
+
+def hold_kernel(acts_hbm, after_hbm, held_ref, sems):
+    del after_hbm
+    rows = held_ref.shape[0] // HOLD_PARTS
+    copies = []
+    for i in range(HOLD_PARTS):
+        at = pl.ds(i * rows, rows)
+        copies.append(pltpu.make_async_copy(acts_hbm.at[at], held_ref.at[at], sems.at[i]))
+    for copy in copies:
+        copy.start()
+    for copy in copies:
+        copy.wait()
+
+
+def hold(acts, after):
+    hbm = pl.BlockSpec(memory_space=pl.ANY)
+    return pl.pallas_call(
+        hold_kernel,
+        out_shape=pltpu.VMEM(acts.shape, BF16),
+        in_specs=[hbm, hbm],
+        out_specs=pl.BlockSpec(memory_space=pltpu.VMEM),
+        scratch_shapes=[pltpu.SemaphoreType.DMA((HOLD_PARTS,))],
+        compiler_params=pltpu.CompilerParams(vmem_limit_bytes=HOLD_LIMIT),
+        cost_estimate=pl.CostEstimate(flops=0, bytes_accessed=4 * acts.size, transcendentals=0),
+    )(acts, after)
+
+
 def on_device(acts, basis):
     rows, cols = acts.shape
     k = basis.shape[1]
-    half = k // 2
+    half = cols // 2
     core = lax.axis_index("core").astype(jnp.int32)
     own = core * half
     other = half - own
 
-    product = lax.dot_general(acts, basis, (((0,), (0,)), ((), ())), preferred_element_type=F32)
-    to_other = lax.dynamic_slice(product, (0, other), (cols, half)).astype(BF16)
-    kept = lax.dynamic_slice(product, (0, own), (cols, half))
+    to_other = half_product(acts, basis, other, BF16)
     from_other = lax.ppermute(to_other, "core", SWAP)
+    kept = half_product(acts, basis, own, F32)
     chip_sum = (kept + from_other.astype(F32)).astype(BF16)
-    piece = exchange_sum(chip_sum.reshape(32, cols // 32, half), xy_groups()).astype(BF16)
-    mine = share(piece, xy_groups()).reshape(cols, half)
+    piece = exchange_sum(chip_sum.reshape(32, cols // 32, LANES), xy_groups()).astype(BF16)
+    mine = share(piece, xy_groups()).reshape(2, half, LANES)
     theirs = lax.ppermute(mine, "core", SWAP)
+    held = hold(acts, piece)
     first = jnp.where(core == 0, mine, theirs)
     second = jnp.where(core == 0, theirs, mine)
-    corange = jnp.concatenate([first, second], axis=1)
+    corange = jnp.concatenate([side_by_side(first), side_by_side(second)], axis=0)
 
-    partial_y = jnp.dot(acts, corange, preferred_element_type=F32).astype(BF16)
+    partial_y = jnp.dot(held, corange, preferred_element_type=F32).astype(BF16)
     summed = exchange_sum(partial_y.reshape(8, rows // 8, k), z_groups())
     scaled = (summed * (1.0 / math.sqrt(N))).astype(BF16)
     range_next = share(scaled, z_groups()).reshape(rows, k)

time: 116 us -> 114 us (0.983)
  Pallas kernels: 0 us -> 7.92 us
  matrix products: 5.2 us -> 1.39 us
  waiting for transfers between devices: 3.41 us -> 0.01 us
  local copies, waits for them, and re-layouts: 3.53 us -> 1 us
    pallas_call x0 -> x3, Pallas kernels: none -> 7.92 us  [the longest x2 5.54 us: half_product(): pl.pallas_call(half_product_kernel, out_shape=pltpu.VMEM((k // LANES, hal...]
    dot_general x2 -> x1, matrix products: 5.2 us -> 1.39 us  [on_device(): partial_y = jnp.dot(held, corange, preferred_element_type=F32).astype(BF16)]
    ppermute x1, waiting for transfers between devices: 1.82 us -> 0.01 us  [on_device(): from_other = lax.ppermute(to_other, 'core', SWAP)]
    ppermute x1, waiting for transfers between devices: 1.59 us -> 0.01 us  [on_device(): theirs = lax.ppermute(mine, 'core', SWAP)]
    unnamed x7 -> x5, local copies, waits for them, and re-layouts: 2.31 us -> 0.81 us
  transfers between devices with their start and end apart: 2 -> 2, of which waited for: 2 -> 0; matrix products, arithmetic and copies ran while one was open for 0% -> 0% of each run, Pallas kernels for 0% -> 5%
where the time goes in v3:
time: 114 us; the launch traced here: 113 us
  blocking collectives  85.4 us (75%)
  starting transfers between devices  15.9 us (14%)
  Pallas kernels  7.92 us (7%)
  matrix products  1.39 us (1%)
    all_to_all x4, blocking collectives, exchange(): return lax.all_to_all(pieces, AXES, 0, 0, axis_index_groups=groups)  85.4 us
    ppermute x1, starting transfers between devices, on_device(): from_other = lax.ppermute(to_other, 'core', SWAP)  8.79 us
    ppermute x1, starting transfers between devices, on_device(): theirs = lax.ppermute(mine, 'core', SWAP)  7.1 us
    pallas_call x2, Pallas kernels, half_product(): pl.pallas_call(half_product_kernel, out_shape=pltpu.VMEM((k // LANES, hal...  5.54 us
    pallas_call x1, Pallas kernels, hold(): pl.pallas_call(hold_kernel, out_shape=pltpu.VMEM(acts.shape, BF16), in_sp...  2.37 us
  transfers between devices with their start and end apart: 2, of which 0 were waited for; matrix products, arithmetic and copies ran while one was open for 0% of the time, Pallas kernels for 5%

profile of v3, /device:TPU:1, one launch (start us, length us, event | category | flops | bytes accessed | tf_op | source)
XLA Modules:
  0.0 112.9 jit_solution(3191181653433987024)
XLA Ops:
  0.6 2.8 %shard_map.42 = bf16[2,1152,128]{2,1,0:T(8,128)(2,1)S(1)} custom-call(s32[1]{0:T(128)} %bitcast.1.start_ref, bf16[1024,2304]{1,0:T(8,128)(2,1)} %acts_hbm.5, bf16[1024,256]{1,0:T(8,128)(2,1)} %basis_hbm.3), custom_call_target="tpu_custom_call" | custom-call | flops 603979776 | bytes 2883584 | tf_op jit(solution)/shard_map/pallas_call | solution.py:73
  3.4 8.8 %collective-permute-start = (bf16[2,1152,128]{2,1,0:T(8,128)(2,1)S(1)}, bf16[2,1152,128]{2,1,0:T(8,128)(2,1)S(1)}, u32[]{:S(2)}, u32[]{:S(2)}) collective-permute-start(bf16[2,1152,128]{2,1,0:T(8,128)(2,1)S(1)} %shard_map.42), channel_id=1, source_target_pairs={{0,8},{8,0},{1,9},{9,1},{2,10},{10,2},{3,11},{11,3},{4,12},{12,4},... | collective-permute-start | bytes 1769480 | tf_op jit(solution)/shard_map/ppermute | solution.py:132
  12.2 2.8 %shard_map.41 = f32[2,1152,128]{2,1,0:T(8,128)S(1)} custom-call(s32[1]{0:T(128)} %bitcast.start_ref, bf16[1024,2304]{1,0:T(8,128)(2,1)} %acts_hbm.5, bf16[1024,256]{1,0:T(8,128)(2,1)} %basis_hbm.3), custom_call_target="tpu_custom_call" | custom-call | flops 603979776 | bytes 2883584 | tf_op jit(solution)/shard_map/pallas_call | solution.py:73
  15.0 0.0 collective-permute-done
  15.0 0.1 add_convert_fusion
  15.1 20.8 %all_to_all.20 = bf16[32,72,128]{2,1,0:T(8,128)(2,1)S(1)} all-to-all(bf16[32,72,128]{2,1,0:T(8,128)(2,1)S(1)} %bitcast.21), channel_id=1, replica_groups={{0,176,352,400,64,240,288,464,128,304,480,16,192,368,416,80,256,432,96,..., dimensions={0} | all-to-all | bytes 1179648 | tf_op jit(solution)/shard_map/all_to_all | solution.py:40
  35.9 0.1 reduce_sum.21.after_hbm
  36.0 0.0 copy-start.1
  36.0 0.1 broadcast_in_dim.4
  36.1 21.1 %all_to_all.21 = bf16[32,72,128]{2,1,0:T(8,128)(2,1)S(1)} all-to-all(bf16[32,72,128]{2,1,0:T(8,128)(2,1)S(1)} %broadcast_in_dim.4), channel_id=1, replica_groups={{0,176,352,400,64,240,288,464,128,304,480,16,192,368,416,80,256,432,96,..., dimensions={0} | all-to-all | bytes 1179648 | tf_op jit(solution)/shard_map/all_to_all | solution.py:40
  57.2 7.1 %collective-permute-start.1 = (bf16[2,1152,128]{2,1,0:T(8,128)(2,1)S(1)}, bf16[2,1152,128]{2,1,0:T(8,128)(2,1)S(1)}, u32[]{:S(2)}, u32[]{:S(2)}) collective-permute-start(bf16[2,1152,128]{2,1,0:T(8,128)(2,1)S(1)} %bitcast.19), channel_id=1, source_target_pairs={{0,8},{8,0},{1,9},{9,1},{2,10},{10,2},{3,11},{11,3},{4,12},{12,4},... | collective-permute-start | bytes 1769480 | tf_op jit(solution)/shard_map/ppermute | solution.py:137
  64.3 0.0 copy-done.1
  64.3 2.4 %shard_map.43 = bf16[1024,2304]{1,0:T(8,128)(2,1)S(1)} custom-call(bf16[1024,2304]{1,0:T(8,128)(2,1)} %acts_hbm.5, bf16[72,128]{1,0:T(8,128)(2,1)} %copy-done.1), custom_call_target="tpu_custom_call" | custom-call | bytes 9437184 | tf_op jit(solution)/shard_map/pallas_call | solution.py:112
  66.7 0.0 collective-permute-done.1
  66.7 0.1 broadcast_select_fusion.1
  66.8 0.1 slice_bitcast_fusion.1
  66.9 0.1 maximum_maximum_fusion
  67.0 0.0 copy-start
  67.0 1.4 %convolution_convert_fusion = bf16[1024,256]{1,0:T(8,128)(2,1)S(1)} fusion(bf16[1024,2304]{1,0:T(8,128)(2,1)S(1)} %shard_map.43, bf16[2304,256]{1,0:T(8,128)(2,1)S(1)} %maximum_maximum_fusion), kind=kOutput, calls=%fused_computation | convolution fusion | flops 1208221696 | bytes 6422528 | tf_op jit(solution)/shard_map/dot_general | solution.py:143
  68.4 0.0 copy-done
  68.4 26.3 %all_to_all.22 = bf16[8,128,256]{2,1,0:T(8,128)(2,1)S(1)} all-to-all(bf16[8,128,256]{2,1,0:T(8,128)(2,1)S(1)} %bitcast.23), channel_id=1, replica_groups={{0,3,6,1,4,7,2,5},{8,13,10,15,12,9,14,11},{16,19,22,17,20,23,18,21},{24..., dimensions={0} | all-to-all | bytes 1048576 | tf_op jit(solution)/shard_map/all_to_all | solution.py:40
  94.7 0.1 convert_reduce_fusion
  94.9 17.3 %all_to_all.23 = bf16[8,128,256]{2,1,0:T(8,128)(2,1)S(1)} all-to-all(bf16[8,128,256]{2,1,0:T(8,128)(2,1)S(1)} %broadcast_in_dim.5), channel_id=1, replica_groups={{0,3,6,1,4,7,2,5},{8,13,10,15,12,9,14,11},{16,19,22,17,20,23,18,21},{24..., dimensions={0} | all-to-all | bytes 1048576 | tf_op jit(solution)/shard_map/all_to_all | solution.py:40
  112.2 0.8 copy.5
  (2 shorter events, 0.0 us)
Async XLA Ops:
  3.4 11.6 %collective-permute-start = (bf16[2,1152,128]{2,1,0:T(8,128)(2,1)S(1)}, bf16[2,1152,128]{2,1,0:T(8,128)(2,1)S(1)}, u32[]{:S(2)}, u32[]{:S(2)}) collective-permute-start(bf16[2,1152,128]{2,1,0:T(8,128)(2,1)S(1)} %shard_map.42), channel_id=1, source_target_pairs={{0,8},{8,0},{1,9},{9,1},{2,10},{10,2},{3,11},{11,3},{4,12},{12,4},... | collective-permute-start | bytes 1769480 | tf_op jit(solution)/shard_map/ppermute | solution.py:132
  36.0 28.3 %copy-start.1 = (bf16[72,128]{1,0:T(8,128)(2,1)}, bf16[72,128]{1,0:T(8,128)(2,1)S(1)}, u32[]{:S(2)}) copy-start(bf16[72,128]{1,0:T(8,128)(2,1)S(1)} %reduce_sum.21.after_hbm) | copy-start | bytes 55300
  57.2 9.5 %collective-permute-start.1 = (bf16[2,1152,128]{2,1,0:T(8,128)(2,1)S(1)}, bf16[2,1152,128]{2,1,0:T(8,128)(2,1)S(1)}, u32[]{:S(2)}, u32[]{:S(2)}) collective-permute-start(bf16[2,1152,128]{2,1,0:T(8,128)(2,1)S(1)} %bitcast.19), channel_id=1, source_target_pairs={{0,8},{8,0},{1,9},{9,1},{2,10},{10,2},{3,11},{11,3},{4,12},{12,4},... | collective-permute-start | bytes 1769480 | tf_op jit(solution)/shard_map/ppermute | solution.py:137
  67.0 1.4 %copy-start = (bf16[2304,256]{1,0:T(8,128)(2,1)}, bf16[2304,256]{1,0:T(8,128)(2,1)S(1)}, u32[]{:S(2)}) copy-start(bf16[2304,256]{1,0:T(8,128)(2,1)S(1)} %maximum_maximum_fusion) | copy-start | bytes 3538948

commit v4 on v3

--- a/solution.py
+++ b/solution.py
@@ -21,15 +21,19 @@
 
 
 def xy_groups():
-    order = [((p // 8 + p) % 4, 3 * p % 8) for p in range(32)]
+    orders = (
+        [(p // 8, 3 * p % 8) for p in range(32)],
+        [(-(p // 8) % 4, 5 * p % 8) for p in range(32)],
+    )
     return [
-        [int(IDS[x, y, core, z]) for x, y in order] for core in range(2) for z in range(8)
+        [int(IDS[x, y, core, z]) for x, y in orders[core]] for core in range(2) for z in range(8)
     ]
 
 
 def z_groups():
+    order = (0, 2, 4, 6, 1, 3, 5, 7)
     return [
-        [int(IDS[x, y, core, (5 if core else 3) * p % 8]) for p in range(8)]
+        [int(IDS[x, y, core, z]) for z in order]
         for x in range(4)
         for y in range(8)
         for core in range(2)

time: 114 us -> 113 us (level)
  the two profiles are of different devices: /device:TPU:1 before, /device:TPU:64 now
where the time goes in v4:
time: 113 us
  blocking collectives  97.4 us (86%)
  Pallas kernels  7.92 us (7%)
  starting transfers between devices  3.83 us (3%)
  matrix products  1.39 us (1%)
    all_to_all x4, blocking collectives, exchange(): return lax.all_to_all(pieces, AXES, 0, 0, axis_index_groups=groups)  97.4 us
    pallas_call x2, Pallas kernels, half_product(): pl.pallas_call(half_product_kernel, out_shape=pltpu.VMEM((k // LANES, hal...  5.54 us
    pallas_call x1, Pallas kernels, hold(): pl.pallas_call(hold_kernel, out_shape=pltpu.VMEM(acts.shape, BF16), in_sp...  2.37 us
  transfers between devices with their start and end apart: 2, of which 0 were waited for; matrix products, arithmetic and copies ran while one was open for 0% of the time, Pallas kernels for 5%

profile of v4, /device:TPU:64, one launch (start us, length us, event | category | flops | bytes accessed | tf_op | source)
XLA Modules:
  0.0 112.8 jit_solution(16846817990906416395)
XLA Ops:
  0.6 2.8 %shard_map.42 = bf16[2,1152,128]{2,1,0:T(8,128)(2,1)S(1)} custom-call(s32[1]{0:T(128)} %bitcast.1.start_ref, bf16[1024,2304]{1,0:T(8,128)(2,1)} %acts_hbm.5, bf16[1024,256]{1,0:T(8,128)(2,1)} %basis_hbm.3), custom_call_target="tpu_custom_call" | custom-call | flops 603979776 | bytes 2883584 | tf_op jit(solution)/shard_map/pallas_call | solution.py:77
  3.4 1.9 %collective-permute-start = (bf16[2,1152,128]{2,1,0:T(8,128)(2,1)S(1)}, bf16[2,1152,128]{2,1,0:T(8,128)(2,1)S(1)}, u32[]{:S(2)}, u32[]{:S(2)}) collective-permute-start(bf16[2,1152,128]{2,1,0:T(8,128)(2,1)S(1)} %shard_map.42), channel_id=1, source_target_pairs={{0,8},{8,0},{1,9},{9,1},{2,10},{10,2},{3,11},{11,3},{4,12},{12,4},... | collective-permute-start | bytes 1769480 | tf_op jit(solution)/shard_map/ppermute | solution.py:136
  5.3 2.8 %shard_map.41 = f32[2,1152,128]{2,1,0:T(8,128)S(1)} custom-call(s32[1]{0:T(128)} %bitcast.start_ref, bf16[1024,2304]{1,0:T(8,128)(2,1)} %acts_hbm.5, bf16[1024,256]{1,0:T(8,128)(2,1)} %basis_hbm.3), custom_call_target="tpu_custom_call" | custom-call | flops 603979776 | bytes 2883584 | tf_op jit(solution)/shard_map/pallas_call | solution.py:77
  8.1 0.0 collective-permute-done
  8.1 0.1 add_convert_fusion
  8.3 29.0 %all_to_all.20 = bf16[32,72,128]{2,1,0:T(8,128)(2,1)S(1)} all-to-all(bf16[32,72,128]{2,1,0:T(8,128)(2,1)S(1)} %bitcast.21), channel_id=1, replica_groups={{0,48,96,16,64,112,32,80,128,176,224,144,192,240,160,208,256,304,352,27..., dimensions={0} | all-to-all | bytes 1179648 | tf_op jit(solution)/shard_map/all_to_all | solution.py:44
  37.2 0.1 reduce_sum.21.after_hbm
  37.3 0.0 copy-start.1
  37.4 0.1 broadcast_in_dim.4
  37.4 23.1 %all_to_all.21 = bf16[32,72,128]{2,1,0:T(8,128)(2,1)S(1)} all-to-all(bf16[32,72,128]{2,1,0:T(8,128)(2,1)S(1)} %broadcast_in_dim.4), channel_id=1, replica_groups={{0,48,96,16,64,112,32,80,128,176,224,144,192,240,160,208,256,304,352,27..., dimensions={0} | all-to-all | bytes 1179648 | tf_op jit(solution)/shard_map/all_to_all | solution.py:44
  60.5 1.9 %collective-permute-start.1 = (bf16[2,1152,128]{2,1,0:T(8,128)(2,1)S(1)}, bf16[2,1152,128]{2,1,0:T(8,128)(2,1)S(1)}, u32[]{:S(2)}, u32[]{:S(2)}) collective-permute-start(bf16[2,1152,128]{2,1,0:T(8,128)(2,1)S(1)} %bitcast.19), channel_id=1, source_target_pairs={{0,8},{8,0},{1,9},{9,1},{2,10},{10,2},{3,11},{11,3},{4,12},{12,4},... | collective-permute-start | bytes 1769480 | tf_op jit(solution)/shard_map/ppermute | solution.py:141
  62.5 0.0 copy-done.1
  62.5 2.4 %shard_map.43 = bf16[1024,2304]{1,0:T(8,128)(2,1)S(1)} custom-call(bf16[1024,2304]{1,0:T(8,128)(2,1)} %acts_hbm.5, bf16[72,128]{1,0:T(8,128)(2,1)} %copy-done.1), custom_call_target="tpu_custom_call" | custom-call | bytes 9437184 | tf_op jit(solution)/shard_map/pallas_call | solution.py:116
  64.9 0.0 collective-permute-done.1
  64.9 0.1 broadcast_select_fusion.1
  65.0 0.1 slice_bitcast_fusion.1
  65.1 0.1 maximum_maximum_fusion
  65.2 0.0 copy-start
  65.2 1.4 %convolution_convert_fusion = bf16[1024,256]{1,0:T(8,128)(2,1)S(1)} fusion(bf16[1024,2304]{1,0:T(8,128)(2,1)S(1)} %shard_map.43, bf16[2304,256]{1,0:T(8,128)(2,1)S(1)} %maximum_maximum_fusion), kind=kOutput, calls=%fused_computation | convolution fusion | flops 1208221696 | bytes 6422528 | tf_op jit(solution)/shard_map/dot_general | solution.py:147
  66.6 0.0 copy-done
  66.6 26.5 %all_to_all.22 = bf16[8,128,256]{2,1,0:T(8,128)(2,1)S(1)} all-to-all(bf16[8,128,256]{2,1,0:T(8,128)(2,1)S(1)} %bitcast.23), channel_id=1, replica_groups={{0,2,4,6,1,3,5,7},{8,10,12,14,9,11,13,15},{16,18,20,22,17,19,21,23},{24..., dimensions={0} | all-to-all | bytes 1048576 | tf_op jit(solution)/shard_map/all_to_all | solution.py:44
  93.1 0.1 convert_reduce_fusion
  93.2 18.8 %all_to_all.23 = bf16[8,128,256]{2,1,0:T(8,128)(2,1)S(1)} all-to-all(bf16[8,128,256]{2,1,0:T(8,128)(2,1)S(1)} %broadcast_in_dim.5), channel_id=1, replica_groups={{0,2,4,6,1,3,5,7},{8,10,12,14,9,11,13,15},{16,18,20,22,17,19,21,23},{24..., dimensions={0} | all-to-all | bytes 1048576 | tf_op jit(solution)/shard_map/all_to_all | solution.py:44
  112.1 0.8 copy.5
  (2 shorter events, 0.0 us)
Async XLA Ops:
  3.4 4.7 %collective-permute-start = (bf16[2,1152,128]{2,1,0:T(8,128)(2,1)S(1)}, bf16[2,1152,128]{2,1,0:T(8,128)(2,1)S(1)}, u32[]{:S(2)}, u32[]{:S(2)}) collective-permute-start(bf16[2,1152,128]{2,1,0:T(8,128)(2,1)S(1)} %shard_map.42), channel_id=1, source_target_pairs={{0,8},{8,0},{1,9},{9,1},{2,10},{10,2},{3,11},{11,3},{4,12},{12,4},... | collective-permute-start | bytes 1769480 | tf_op jit(solution)/shard_map/ppermute | solution.py:136
  37.3 25.1 %copy-start.1 = (bf16[72,128]{1,0:T(8,128)(2,1)}, bf16[72,128]{1,0:T(8,128)(2,1)S(1)}, u32[]{:S(2)}) copy-start(bf16[72,128]{1,0:T(8,128)(2,1)S(1)} %reduce_sum.21.after_hbm) | copy-start | bytes 55300
  60.5 4.3 %collective-permute-start.1 = (bf16[2,1152,128]{2,1,0:T(8,128)(2,1)S(1)}, bf16[2,1152,128]{2,1,0:T(8,128)(2,1)S(1)}, u32[]{:S(2)}, u32[]{:S(2)}) collective-permute-start(bf16[2,1152,128]{2,1,0:T(8,128)(2,1)S(1)} %bitcast.19), channel_id=1, source_target_pairs={{0,8},{8,0},{1,9},{9,1},{2,10},{10,2},{3,11},{11,3},{4,12},{12,4},... | collective-permute-start | bytes 1769480 | tf_op jit(solution)/shard_map/ppermute | solution.py:141
  65.2 1.4 %copy-start = (bf16[2304,256]{1,0:T(8,128)(2,1)}, bf16[2304,256]{1,0:T(8,128)(2,1)S(1)}, u32[]{:S(2)}) copy-start(bf16[2304,256]{1,0:T(8,128)(2,1)S(1)} %maximum_maximum_fusion) | copy-start | bytes 3538948

commit v5 on v4

--- a/solution.py
+++ b/solution.py
@@ -20,16 +20,6 @@
 IDS = np.arange(512).reshape(SIZES)
 
 
-def xy_groups():
-    orders = (
-        [(p // 8, 3 * p % 8) for p in range(32)],
-        [(-(p // 8) % 4, 5 * p % 8) for p in range(32)],
-    )
-    return [
-        [int(IDS[x, y, core, z]) for x, y in orders[core]] for core in range(2) for z in range(8)
-    ]
-
-
 def z_groups():
     order = (0, 2, 4, 6, 1, 3, 5, 7)
     return [
@@ -37,6 +27,22 @@
         for x in range(4)
         for y in range(8)
         for core in range(2)
+    ]
+
+
+def x_groups():
+    return [
+        [int(IDS[(3 * x if core else x) % 4, y, core, z]) for x in range(4)]
+        for y in range(8)
+        for core in range(2)
+        for z in range(8)
+    ]
+
+
+def y_groups():
+    order = (0, 2, 4, 6, 1, 3, 5, 7)
+    return [
+        [int(IDS[x, y, core, z]) for y in order] for x in range(4) for core in range(2) for z in range(8)
     ]
 
 
@@ -136,8 +142,10 @@
     from_other = lax.ppermute(to_other, "core", SWAP)
     kept = half_product(acts, basis, own, F32)
     chip_sum = (kept + from_other.astype(F32)).astype(BF16)
-    piece = exchange_sum(chip_sum.reshape(32, cols // 32, LANES), xy_groups()).astype(BF16)
-    mine = share(piece, xy_groups()).reshape(2, half, LANES)
+    over_x = exchange_sum(chip_sum.reshape(4, cols // 4, LANES), x_groups()).astype(BF16)
+    piece = exchange_sum(over_x.reshape(8, cols // 32, LANES), y_groups()).astype(BF16)
+    row = share(piece, y_groups()).reshape(cols // 4, LANES)
+    mine = share(row, x_groups()).reshape(2, half, LANES)
     theirs = lax.ppermute(mine, "core", SWAP)
     held = hold(acts, piece)
     first = jnp.where(core == 0, mine, theirs)

time: 113 us -> 113 us (level)
  the two profiles are of different devices: /device:TPU:64 before, /device:TPU:72 now
where the time goes in v5:
time: 113 us
  blocking collectives  97.1 us (86%)
  Pallas kernels  7.92 us (7%)
  starting transfers between devices  3.83 us (3%)
  matrix products  1.39 us (1%)
    all_to_all x6, blocking collectives, exchange(): return lax.all_to_all(pieces, AXES, 0, 0, axis_index_groups=groups)  97.1 us
    pallas_call x2, Pallas kernels, half_product(): pl.pallas_call(half_product_kernel, out_shape=pltpu.VMEM((k // LANES, hal...  5.54 us
    pallas_call x1, Pallas kernels, hold(): pl.pallas_call(hold_kernel, out_shape=pltpu.VMEM(acts.shape, BF16), in_sp...  2.37 us
  transfers between devices with their start and end apart: 2, of which 0 were waited for; matrix products, arithmetic and copies ran while one was open for 0% of the time, Pallas kernels for 5%

profile of v5, /device:TPU:72, one launch (start us, length us, event | category | flops | bytes accessed | tf_op | source)
XLA Modules:
  0.0 112.6 jit_solution(16806657965379498513)
XLA Ops:
  0.6 2.8 %shard_map.42 = bf16[2,1152,128]{2,1,0:T(8,128)(2,1)S(1)} custom-call(s32[1]{0:T(128)} %bitcast.1.start_ref, bf16[1024,2304]{1,0:T(8,128)(2,1)} %acts_hbm.5, bf16[1024,256]{1,0:T(8,128)(2,1)} %basis_hbm.3), custom_call_target="tpu_custom_call" | custom-call | flops 603979776 | bytes 2883584 | tf_op jit(solution)/shard_map/pallas_call | solution.py:83
  3.4 1.9 %collective-permute-start = (bf16[2,1152,128]{2,1,0:T(8,128)(2,1)S(1)}, bf16[2,1152,128]{2,1,0:T(8,128)(2,1)S(1)}, u32[]{:S(2)}, u32[]{:S(2)}) collective-permute-start(bf16[2,1152,128]{2,1,0:T(8,128)(2,1)S(1)} %shard_map.42), channel_id=1, source_target_pairs={{0,8},{8,0},{1,9},{9,1},{2,10},{10,2},{3,11},{11,3},{4,12},{12,4},... | collective-permute-start | bytes 1769480 | tf_op jit(solution)/shard_map/ppermute | solution.py:142
  5.3 2.8 %shard_map.41 = f32[2,1152,128]{2,1,0:T(8,128)S(1)} custom-call(s32[1]{0:T(128)} %bitcast.start_ref, bf16[1024,2304]{1,0:T(8,128)(2,1)} %acts_hbm.5, bf16[1024,256]{1,0:T(8,128)(2,1)} %basis_hbm.3), custom_call_target="tpu_custom_call" | custom-call | flops 603979776 | bytes 2883584 | tf_op jit(solution)/shard_map/pallas_call | solution.py:83
  8.1 0.0 collective-permute-done
  8.1 0.1 add_convert_fusion
  8.3 14.9 %all_to_all.30 = bf16[4,576,128]{2,1,0:T(8,128)(2,1)S(1)} all-to-all(bf16[4,576,128]{2,1,0:T(8,128)(2,1)S(1)} %bitcast.23), channel_id=1, replica_groups={{0,128,256,384},{1,129,257,385},{2,130,258,386},{3,131,259,387},{4,132,..., dimensions={0} | all-to-all | bytes 1179648 | tf_op jit(solution)/shard_map/all_to_all | solution.py:50
  23.2 0.1 reduce_sum.33
  23.3 15.1 %all_to_all.31 = bf16[8,72,128]{2,1,0:T(8,128)(2,1)S(1)} all-to-all(bf16[8,72,128]{2,1,0:T(8,128)(2,1)S(1)} %bitcast.25), channel_id=1, replica_groups={{0,32,64,96,16,48,80,112},{1,33,65,97,17,49,81,113},{2,34,66,98,18,50,8..., dimensions={0} | all-to-all | bytes 294912 | tf_op jit(solution)/shard_map/all_to_all | solution.py:50
  38.5 0.0 copy-start.1
  38.5 10.9 %all_to_all.32 = bf16[8,72,128]{2,1,0:T(8,128)(2,1)S(1)} all-to-all(bf16[8,72,128]{2,1,0:T(8,128)(2,1)S(1)} %broadcast_in_dim.8), channel_id=1, replica_groups={{0,32,64,96,16,48,80,112},{1,33,65,97,17,49,81,113},{2,34,66,98,18,50,8..., dimensions={0} | all-to-all | bytes 294912 | tf_op jit(solution)/shard_map/all_to_all | solution.py:50
  49.4 0.1 broadcast_in_dim.10
  49.5 10.8 %all_to_all.33 = bf16[4,576,128]{2,1,0:T(8,128)(2,1)S(1)} all-to-all(bf16[4,576,128]{2,1,0:T(8,128)(2,1)S(1)} %broadcast_in_dim.10), channel_id=1, replica_groups={{0,128,256,384},{1,129,257,385},{2,130,258,386},{3,131,259,387},{4,132,..., dimensions={0} | all-to-all | bytes 1179648 | tf_op jit(solution)/shard_map/all_to_all | solution.py:50
  60.3 0.0 copy-done.1
  60.3 1.9 %collective-permute-start.1 = (bf16[2,1152,128]{2,1,0:T(8,128)(2,1)S(1)}, bf16[2,1152,128]{2,1,0:T(8,128)(2,1)S(1)}, u32[]{:S(2)}, u32[]{:S(2)}) collective-permute-start(bf16[2,1152,128]{2,1,0:T(8,128)(2,1)S(1)} %bitcast.21), channel_id=1, source_target_pairs={{0,8},{8,0},{1,9},{9,1},{2,10},{10,2},{3,11},{11,3},{4,12},{12,4},... | collective-permute-start | bytes 1769480 | tf_op jit(solution)/shard_map/ppermute | solution.py:149
  62.2 2.4 %shard_map.43 = bf16[1024,2304]{1,0:T(8,128)(2,1)S(1)} custom-call(bf16[1024,2304]{1,0:T(8,128)(2,1)} %acts_hbm.5, bf16[72,128]{1,0:T(8,128)(2,1)} %copy-done.1), custom_call_target="tpu_custom_call" | custom-call | bytes 9437184 | tf_op jit(solution)/shard_map/pallas_call | solution.py:122
  64.6 0.0 collective-permute-done.1
  64.6 0.1 broadcast_select_fusion.1
  64.7 0.1 slice_bitcast_fusion.1
  64.8 0.1 maximum_maximum_fusion
  64.9 0.0 copy-start
  64.9 1.4 %convolution_convert_fusion = bf16[1024,256]{1,0:T(8,128)(2,1)S(1)} fusion(bf16[1024,2304]{1,0:T(8,128)(2,1)S(1)} %shard_map.43, bf16[2304,256]{1,0:T(8,128)(2,1)S(1)} %maximum_maximum_fusion), kind=kOutput, calls=%fused_computation | convolution fusion | flops 1208221696 | bytes 6422528 | tf_op jit(solution)/shard_map/dot_general | solution.py:155
  66.3 0.0 copy-done
  66.4 26.5 %all_to_all.34 = bf16[8,128,256]{2,1,0:T(8,128)(2,1)S(1)} all-to-all(bf16[8,128,256]{2,1,0:T(8,128)(2,1)S(1)} %bitcast.27), channel_id=1, replica_groups={{0,2,4,6,1,3,5,7},{8,10,12,14,9,11,13,15},{16,18,20,22,17,19,21,23},{24..., dimensions={0} | all-to-all | bytes 1048576 | tf_op jit(solution)/shard_map/all_to_all | solution.py:50
  92.8 0.1 convert_reduce_fusion
  93.0 18.8 %all_to_all.35 = bf16[8,128,256]{2,1,0:T(8,128)(2,1)S(1)} all-to-all(bf16[8,128,256]{2,1,0:T(8,128)(2,1)S(1)} %broadcast_in_dim.22), channel_id=1, replica_groups={{0,2,4,6,1,3,5,7},{8,10,12,14,9,11,13,15},{16,18,20,22,17,19,21,23},{24..., dimensions={0} | all-to-all | bytes 1048576 | tf_op jit(solution)/shard_map/all_to_all | solution.py:50
  111.8 0.8 copy.5
  (4 shorter events, 0.1 us)
Async XLA Ops:
  3.4 4.7 %collective-permute-start = (bf16[2,1152,128]{2,1,0:T(8,128)(2,1)S(1)}, bf16[2,1152,128]{2,1,0:T(8,128)(2,1)S(1)}, u32[]{:S(2)}, u32[]{:S(2)}) collective-permute-start(bf16[2,1152,128]{2,1,0:T(8,128)(2,1)S(1)} %shard_map.42), channel_id=1, source_target_pairs={{0,8},{8,0},{1,9},{9,1},{2,10},{10,2},{3,11},{11,3},{4,12},{12,4},... | collective-permute-start | bytes 1769480 | tf_op jit(solution)/shard_map/ppermute | solution.py:142
  38.5 21.8 %copy-start.1 = (bf16[72,128]{1,0:T(8,128)(2,1)}, bf16[72,128]{1,0:T(8,128)(2,1)S(1)}, u32[]{:S(2)}) copy-start(bf16[72,128]{1,0:T(8,128)(2,1)S(1)} %reduce_sum.34.after_hbm) | copy-start | bytes 55300
  60.3 4.3 %collective-permute-start.1 = (bf16[2,1152,128]{2,1,0:T(8,128)(2,1)S(1)}, bf16[2,1152,128]{2,1,0:T(8,128)(2,1)S(1)}, u32[]{:S(2)}, u32[]{:S(2)}) collective-permute-start(bf16[2,1152,128]{2,1,0:T(8,128)(2,1)S(1)} %bitcast.21), channel_id=1, source_target_pairs={{0,8},{8,0},{1,9},{9,1},{2,10},{10,2},{3,11},{11,3},{4,12},{12,4},... | collective-permute-start | bytes 1769480 | tf_op jit(solution)/shard_map/ppermute | solution.py:149
  64.9 1.4 %copy-start = (bf16[2304,256]{1,0:T(8,128)(2,1)}, bf16[2304,256]{1,0:T(8,128)(2,1)S(1)}, u32[]{:S(2)}) copy-start(bf16[2304,256]{1,0:T(8,128)(2,1)S(1)} %maximum_maximum_fusion) | copy-start | bytes 3538948
